TPU v7x, 32 devices: a whole 2x2x4 slice. The times are simulated.
32 devices in a mesh: node: 4 (over z), dev: 8 (over y, x, core).
Axes of the slice: x: 2, y: 2, z: 4, core: 2. Of those that a mesh axis runs over, the one named last changes fastest.
Arguments:
- tables: bfloat16 [64, 2048, 256], P(('node', 'dev')), may hold values from -0.5 to 0.5
- ids: int32 [64, 512, 8], P(None, ('node', 'dev')), may hold values from 0 to 2047
- counts: int32 [64, 32], P(('node', 'dev')), may hold values from 1 to 12, as said below
Outputs:
- interaction: bfloat16 [512, 64, 64], P(('node', 'dev'))
Inputs may be any that keep to these rules, and one draw needn't show every extreme that they name: `counts`: every owner has some feature with exactly 12 live samples, and each feature reaches 12 for some owner. `ids`: row indices may be packed several to a word wherever they travel.
All inputs are finite; a program needn't handle non-finite values.
Results may differ from a plain program's by a relative error of at most 0.0049.
Values may be sent and summed in bfloat16 or wider, within the bound.
A program may use at most 64 MiB of HBM per device.

v0:
```python
import jax
import jax.numpy as jnp
from jax import lax
from jax.sharding import PartitionSpec as P


def pair_products(received):
    return jnp.einsum(
        "rfd,rgd->rfg", received, received, preferred_element_type=jnp.float32
    ).astype(jnp.bfloat16)


def pool_blocks(table, index):
    total = index.shape[0]
    height = table.shape[0]
    bagged = index.shape[1]
    step = 512
    parted = index.reshape(total // step, step, bagged)

    def one_block(piece):
        row_ids = lax.broadcasted_iota(jnp.int32, (step, height), 1)
        tally = jnp.zeros((step, height), jnp.float32)
        for entry in range(bagged):
            tally = tally + (piece[:, entry][:, None] == row_ids).astype(jnp.float32)
        summed = jnp.dot(tally.astype(jnp.bfloat16), table, preferred_element_type=jnp.float32)
        return summed.astype(jnp.bfloat16)

    summed = lax.map(one_block, parted)
    return summed.reshape(total, table.shape[1])


def shards(tables, ids, counts):
    held = tables.shape[0]
    owned = ids.shape[1]
    width = tables.shape[2]
    groups = lax.axis_size("node")
    members = lax.axis_size("dev")
    owners = groups * members
    mine = lax.all_to_all(ids, ("node", "dev"), split_axis=0, concat_axis=1, tiled=True)
    total = mine.shape[1]
    position = lax.broadcasted_iota(jnp.int32, (total,), 0)
    local = position % owned
    owner = position // owned
    columns = []
    for feature in range(held):
        summed = pool_blocks(tables[feature], mine[feature])
        live = local < counts[feature][owner]
        columns.append(jnp.where(live[:, None], summed, jnp.zeros_like(summed)))
    pooled = jnp.stack(columns, axis=1)
    outgoing = pooled.reshape(owners, owned, held, width)
    return pair_products(
        lax.all_to_all(outgoing, ("node", "dev"), split_axis=0, concat_axis=2, tiled=True)[0]
    )


def solution(mesh):
    return jax.shard_map(
        shards,
        mesh=mesh,
        in_specs=(
            P(("node", "dev"), None, None),
            P(None, ("node", "dev"), None),
            P(("node", "dev"), None),
        ),
        out_specs=P(("node", "dev"), None, None),
        check_vma=False,
    )
```

profile of v0, /device:TPU:0, one launch (start us, length us, event | category | flops | bytes accessed | tf_op | source)
XLA Modules:
  0.0 91.3 jit_solution(12182077617184877109)
XLA Ops:
  0.0 1.1 %copy.16 = s32[64,16,8]{1,2,0:T(8,128)S(1)} copy(s32[64,16,8]{0,2,1:T(8,128)} %param.4) | data formatting | bytes 65536 | tf_op args[1]
  1.1 0.8 reshape.443
  1.9 7.3 %all-to-all-start = ((s32[32,1,256]{2,1,0:T(1,128)}), s32[32,1,256]{2,1,0:T(1,128)S(1)}, u32[]{:S(2)}, u32[]{:S(2)}) async-start(s32[32,1,256]{2,1,0:T(1,128)} %reshape.443), calls=%async_computation | async-start | bytes 65536 | tf_op jit(solution)/shard_map/all_to_all | solution.py:39
  10.1 1.6 %fusion.20 = (s32[1,1]{1,0:T(1,128)}, s32[1,1]{1,0:T(1,128)}, s32[1,1]{1,0:T(1,128)}, s32[1,1]{1,0:T(1,128)}, s32[1,1]{1,0:T(1,128)}, /*index=5*/s32[1,1]{1,0:T(1,128)}, s32[1,1]{1,0:T(1,128)}) fusion(s32[2,32]{1,0:T(2,128)} %param.5), kind=kLoop, calls=%fused_computation.88 | loop fusion | bytes 56 | tf_op jit(solution)/shard_map/gather | solution.py:47
  11.7 2.1 %fusion.19 = (s32[1,1]{1,0:T(1,128)}, s32[1,1]{1,0:T(1,128)}, s32[1,1]{1,0:T(1,128)}, s32[1,1]{1,0:T(1,128)}, s32[1,1]{1,0:T(1,128)}, /*index=5*/s32[1,1]{1,0:T(...) fusion(s32[2,32]{1,0:T(2,128)} %param.5), kind=kLoop, calls=%fused_computation.87 | loop fusion | bytes 152 | tf_op jit(solution)/shard_map/gather | solution.py:47
  13.8 2.1 %fusion.17 = (s32[1,1]{1,0:T(1,128)}, s32[1,1]{1,0:T(1,128)}, s32[1,1]{1,0:T(1,128)}, s32[1,1]{1,0:T(1,128)}, s32[1,1]{1,0:T(1,128)}, /*index=5*/s32[1,1]{1,0:T(...) fusion(s32[2,32]{1,0:T(2,128)} %param.5), kind=kLoop, calls=%fused_computation.85 | loop fusion | bytes 152 | tf_op jit(solution)/shard_map/gather | solution.py:47
  15.9 2.1 %fusion.18 = (s32[1,1]{1,0:T(1,128)}, s32[1,1]{1,0:T(1,128)}, s32[1,1]{1,0:T(1,128)}, s32[1,1]{1,0:T(1,128)}, s32[1,1]{1,0:T(1,128)}, /*index=5*/s32[1,1]{1,0:T(...) fusion(s32[2,32]{1,0:T(2,128)} %param.5), kind=kLoop, calls=%fused_computation.86 | loop fusion | bytes 152 | tf_op jit(solution)/shard_map/gather | solution.py:47
  18.0 4.3 %compare_select_fusion.1 = s32[512,1]{0,1:T(1,128)S(1)} fusion(s32[]{:T(128)} %bitcast.25, s32[]{:T(128)} %bitcast.26, s32[]{:T(128)} %bitcast.27, s32[]{:T(128)} %bitcast.28, s32[]{:T(128)} %bitcast.29, s32[]{:T(128)} %bitcast.31, s32[]{:T(128)} %bitcast.30), kind=kLoop, calls=%fused_computation.65 | loop fusion | flops 11776 | bytes 2076 | tf_op jit(solution)/shard_map/gather | solution.py:47
  22.3 15.7 %select_select_fusion.1 = s32[512]{0:T(512)S(1)} fusion(pred[512]{0:T(512)(128)(4,1)S(1)} %compare_reduce_fusion, pred[512]{0:T(512)(128)(4,1)S(1)} %compare_reduce_fusion.1, pred[512]{0:T(512)(128)(4,1)S(1)} %compare_reduce_fusion.2, pred[512]{0:T(512)(128)(4,1)S(1)} %compare_reduce_fusion.3, pred[512]{0:T(512)(128)(4,1)S(1)} %compare_reduce_fusion.4, ...), kind=kLoop, calls=%fused_computation.81 | loop fusion | flops 12800 | bytes 16996 | tf_op jit(solution)/shard_map/gather | solution.py:47
  38.1 0.1 gather.11
  38.2 4.3 %compare_select_fusion.2 = s32[512,1]{0,1:T(1,128)S(1)} fusion(s32[]{:T(128)} %bitcast.71, s32[]{:T(128)} %bitcast.72, s32[]{:T(128)} %bitcast.73, s32[]{:T(128)} %bitcast.74, s32[]{:T(128)} %bitcast.75, s32[]{:T(128)} %bitcast.77, s32[]{:T(128)} %bitcast.76), kind=kLoop, calls=%fused_computation.66 | loop fusion | flops 11776 | bytes 2076 | tf_op jit(solution)/shard_map/gather | solution.py:47
  42.5 15.5 %select_select_fusion = s32[512]{0:T(512)S(1)} fusion(pred[512]{0:T(512)(128)(4,1)S(1)} %compare_reduce_fusion, pred[512]{0:T(512)(128)(4,1)S(1)} %compare_reduce_fusion.1, pred[512]{0:T(512)(128)(4,1)S(1)} %compare_reduce_fusion.2, pred[512]{0:T(512)(128)(4,1)S(1)} %compare_reduce_fusion.3, pred[512]{0:T(512)(128)(4,1)S(1)} %compare_reduce_fusion.4, ...), kind=kLoop, calls=%fused_computation.80 | loop fusion | flops 12800 | bytes 16996 | tf_op jit(solution)/shard_map/gather | solution.py:47
  58.0 0.1 gather.13
  58.1 0.0 all-to-all-done
  58.1 0.5 broadcast.539
  58.6 0.7 reduce.50
  59.4 0.1 reshape.444
  59.6 0.1 squeeze.25
  59.7 0.1 squeeze.28
  59.9 4.4 %fusion.2 = bf16[512,256]{1,0:T(8,128)(2,1)S(1)} fusion(s32[512]{0:T(512)S(1)} %bitcast.128, s32[512]{0:T(512)S(1)} %bitcast.129, s32[512]{0:T(512)S(1)} %bitcast.130, s32[512]{0:T(512)S(1)} %bitcast.131, s32[512]{0:T(512)S(1)} %bitcast.132, s32[512]{0:T(512)S(1)} %bitcast.133, s32[512]{0:T(512)S(1)} %bitcast.134, s32[512]{0:T(512)S(1)} %bitcast.127, ...), kind=kOutput, calls=%fused_computation.20 | convolution fusion | flops 562167808 | bytes 1327104 | tf_op jit(solution)/shard_map/while/body/eval_jaxpr/dot_general | solution.py:25
  64.2 4.4 %fusion.3 = bf16[512,256]{1,0:T(8,128)(2,1)S(1)} fusion(s32[512]{0:T(512)S(1)} %bitcast.120, s32[512]{0:T(512)S(1)} %bitcast.121, s32[512]{0:T(512)S(1)} %bitcast.122, s32[512]{0:T(512)S(1)} %bitcast.123, s32[512]{0:T(512)S(1)} %bitcast.124, s32[512]{0:T(512)S(1)} %bitcast.125, s32[512]{0:T(512)S(1)} %bitcast.126, s32[512]{0:T(512)S(1)} %bitcast.119, ...), kind=kOutput, calls=%fused_computation.21 | convolution fusion | flops 562167808 | bytes 1327104 | tf_op jit(solution)/shard_map/while/body/eval_jaxpr/dot_general | solution.py:25
  68.7 0.2 broadcast_select_fusion
  68.9 21.2 %all_to_all.30 = bf16[32,16,2,256]{3,1,2,0:T(8,128)(2,1)S(1)} all-to-all(bf16[32,16,2,256]{3,1,2,0:T(8,128)(2,1)S(1)} %pad_maximum_fusion), channel_id=1, replica_groups=mesh['node'=4,'dev'=8] {'node','dev'}, dimensions={0} | all-to-all | bytes 1048576 | tf_op jit(solution)/shard_map/all_to_all | solution.py:52
  90.1 1.1 %convolution_convert_fusion = bf16[16,64,64]{2,1,0:T(8,128)(2,1)} fusion(bf16[16,64,256]{2,0,1:T(8,128)(2,1)S(1)} %bitcast.114), kind=kOutput, calls=%fused_computation.22 | convolution fusion | flops 33619968 | bytes 655360 | tf_op jit(solution)/shard_map/rfd,rgd->rfg/dot_general | solution.py:8
  (35 shorter events, 1.0 us)
Async XLA Ops:
  0.0 59.9 %copy-start = (bf16[2,2048,256]{2,1,0:T(8,128)(2,1)S(1)}, bf16[2,2048,256]{2,1,0:T(8,128)(2,1)}, u32[]{:S(2)}) copy-start(bf16[2,2048,256]{2,1,0:T(8,128)(2,1)} %param.3) | copy-start | bytes 6291460
  1.9 56.2 %all-to-all-start = ((s32[32,1,256]{2,1,0:T(1,128)}), s32[32,1,256]{2,1,0:T(1,128)S(1)}, u32[]{:S(2)}, u32[]{:S(2)}) async-start(s32[32,1,256]{2,1,0:T(1,128)} %reshape.443), calls=%async_computation | async-start | bytes 65536 | tf_op jit(solution)/shard_map/all_to_all | solution.py:39
where the time goes:
time: 92.1 us; the launch traced here: 91.3 us
  other arithmetic  41.8 us (45%)
  blocking collectives  21.2 us (23%)
  local copies, waits for them, and re-layouts  10.9 us (12%)
  matrix products  9.9 us (11%)
  starting transfers between devices  7.3 us (8%)
    gather x29, other arithmetic, shards(): live = local < counts[feature][owner]  40.7 us
    all_to_all x1, blocking collectives, shards(): lax.all_to_all(outgoing, ('node', 'dev'), split_axis=0, concat_axis=2, ti...  21.2 us
    dot_general x2, matrix products, one_block(): jnp.dot(tally.astype(jnp.bfloat16), table, preferred_element_type=jnp.flo...  8.78 us
    gather x6, local copies, waits for them, and re-layouts, shards(): live = local < counts[feature][owner]  8.06 us
    all_to_all x1, starting transfers between devices, shards(): lax.all_to_all(ids, ('node', 'dev'), split_axis=0, concat_axis=1, tiled=T...  7.3 us
    unnamed x5, local copies, waits for them, and re-layouts  2.03 us
  transfers between devices with their start and end apart: 1, of which 0 were waited for; matrix products, arithmetic and copies ran while one was open for 53% of the time, Pallas kernels for 0%

commit v1 on v0

v1 whole, which is shorter than its diff:
```python
import functools

import jax
import jax.numpy as jnp
from jax import lax
from jax.experimental import pallas as pl
from jax.experimental.pallas import tpu as pltpu
from jax.sharding import PartitionSpec as P

LIVE = 12
LANES = 128
MESH = pl.DeviceIdType.MESH


def kernel(
    groups, members, owned, bagged,
    table_ref, ids_ref, counts_ref, out_ref,
    id_got, tally, staged, outgoing, received, vectors,
    id_send, id_recv, row_send, row_recv,
):
    total = groups * members
    held, height, width = table_ref.shape
    halves = width // LANES
    lines = held * halves * LIVE
    node = lax.axis_index("node")
    dev = lax.axis_index("dev")
    me = node * members + dev

    def place(device):
        return (device // members, lax.rem(device, members))

    def id_copy(device, source):
        return pltpu.make_async_remote_copy(
            src_ref=ids_ref.at[device],
            dst_ref=id_got.at[source],
            send_sem=id_send.at[device],
            recv_sem=id_recv.at[source],
            device_id=place(device),
            device_id_type=MESH,
        )

    def row_copy(device, source):
        return pltpu.make_async_remote_copy(
            src_ref=outgoing.at[device],
            dst_ref=received.at[source],
            send_sem=row_send.at[device],
            recv_sem=row_recv.at[source],
            device_id=place(device),
            device_id_type=MESH,
        )

    barrier = pltpu.get_barrier_semaphore()

    @pl.loop(1, total)
    def _(step):
        pl.semaphore_signal(
            barrier, inc=1, device_id=place(lax.rem(me + step, total)), device_id_type=MESH
        )

    pl.semaphore_wait(barrier, total - 1)

    @pl.loop(1, total)
    def _(step):
        id_copy(lax.rem(me + step, total), me).start()

    id_got[me] = ids_ref[me]

    spread = (
        lax.rem(lax.broadcasted_iota(jnp.int32, (2 * LANES, bagged * LANES), 0), bagged)
        == lax.broadcasted_iota(jnp.int32, (2 * LANES, bagged * LANES), 1) // LANES
    ).astype(jnp.float32).astype(jnp.bfloat16)
    sample = lax.broadcasted_iota(jnp.int32, (LIVE, members, LANES), 0)
    on_lane = lax.broadcasted_iota(jnp.int32, (LIVE, members, LANES), 2) // bagged == sample
    rows = LIVE * members

    for turn in range(groups):
        group = lax.rem(node + turn + 1, groups)
        first = group * members

        def wait_ids(member):
            id_copy(first + member, first + member).wait_recv()

        if turn < groups - 1:
            @pl.loop(0, members)
            def _(member):
                wait_ids(member)
        else:
            @pl.loop(1, members)
            def _(step):
                wait_ids(lax.rem(dev + step, members))

        for feature in range(held):
            index = id_got[pl.ds(first, members), feature, :]
            high = jnp.where(on_lane, (index - (index & 15))[None], 0)
            low = jnp.where(on_lane, (index & 15)[None], 0)
            both = jnp.concatenate(
                [high.reshape(rows, LANES), low.reshape(rows, LANES)], axis=1
            ).astype(jnp.float32).astype(jnp.bfloat16)
            wide = jnp.dot(both, spread, preferred_element_type=jnp.float32)
            wide = wide.astype(jnp.int32).astype(jnp.int16)
            number = lax.broadcasted_iota(jnp.int32, (16, height), 1).astype(jnp.int16)
            for part in range(rows // 16):
                count = jnp.zeros((16, height), jnp.bfloat16)
                for entry in range(bagged):
                    piece = wide[part * 16:(part + 1) * 16, entry * LANES:(entry + 1) * LANES]
                    piece = jnp.concatenate([piece] * (height // LANES), axis=1)
                    count = count + jnp.where(
                        piece == number, jnp.ones((), jnp.bfloat16), jnp.zeros((), jnp.bfloat16)
                    )
                tally[part * 16:(part + 1) * 16, :] = count
            pooled = jnp.dot(
                tally[...], table_ref[feature], preferred_element_type=jnp.float32
            )
            limit = counts_ref[pl.ds(first, members), feature, :]
            for half in range(halves):
                for s in range(LIVE):
                    piece = pooled[s * members:(s + 1) * members, half * LANES:(half + 1) * LANES]
                    line = (feature * halves + half) * LIVE + s
                    staged[pl.ds(line, members, stride=lines), :] = jnp.where(s < limit, piece, 0.0)
        outgoing[pl.ds(first, members)] = (
            staged[...].reshape(members, lines, LANES).astype(jnp.bfloat16)
        )

        if turn < groups - 1:
            @pl.loop(0, members)
            def _(step):
                row_copy(first + lax.rem(dev + step, members), me).start()
        else:
            @pl.loop(1, members)
            def _(step):
                row_copy(first + lax.rem(dev + step, members), me).start()

    received[me] = outgoing[me]
    out_ref[LIVE:] = jnp.zeros_like(out_ref[LIVE:])

    for turn in range(groups):
        group = lax.rem(node + 2 * groups - turn - 1, groups)
        first = group * members
        if turn < groups - 1:
            @pl.loop(0, members)
            def _(member):
                row_copy(first + member, first + member).wait_recv()
        else:
            @pl.loop(1, members)
            def _(step):
                source = first + lax.rem(dev + step, members)
                row_copy(source, source).wait_recv()
        staged[...] = (
            received[pl.ds(first, members)].astype(jnp.float32).reshape(members * lines, LANES)
        )
        for feature in range(held):
            for half in range(halves):
                for s in range(LIVE):
                    line = (feature * halves + half) * LIVE + s
                    vectors[s, half, group, pl.ds(feature, members, stride=held), :] = (
                        staged[pl.ds(line, members, stride=lines), :]
                    )

    for s in range(LIVE):
        mine = jnp.concatenate(
            [vectors[s, half].reshape(total * held, LANES) for half in range(halves)], axis=1
        ).astype(jnp.bfloat16)
        out_ref[s] = lax.dot_general(
            mine, mine, (((1,), (1,)), ((), ())), preferred_element_type=jnp.float32
        ).astype(jnp.bfloat16)

    @pl.loop(1, total)
    def _(step):
        device = lax.rem(me + step, total)
        id_copy(device, me).wait_send()
        row_copy(device, me).wait_send()


def shards(tables, ids, counts):
    held, height, width = tables.shape
    features, owned, bagged = ids.shape
    groups = lax.axis_size("node")
    members = lax.axis_size("dev")
    total = groups * members
    lines = held * (width // LANES) * LIVE
    index = ids.reshape(total, held, owned * bagged)
    limits = jnp.broadcast_to(counts.T[:, :, None], (total, held, LANES))
    return pl.pallas_call(
        functools.partial(kernel, groups, members, owned, bagged),
        out_shape=jax.ShapeDtypeStruct((owned, features, features), jnp.bfloat16),
        in_specs=[pl.BlockSpec(memory_space=pltpu.VMEM)] * 3,
        out_specs=pl.BlockSpec(memory_space=pltpu.VMEM),
        scratch_shapes=[
            pltpu.VMEM((total, held, LANES), jnp.int32),
            pltpu.VMEM((LIVE * members, height), jnp.bfloat16),
            pltpu.VMEM((members * lines, LANES), jnp.float32),
            pltpu.VMEM((total, lines, LANES), jnp.bfloat16),
            pltpu.VMEM((total, lines, LANES), jnp.bfloat16),
            pltpu.VMEM((LIVE, width // LANES, groups, members * held, LANES), jnp.float32),
            pltpu.SemaphoreType.DMA((total,)),
            pltpu.SemaphoreType.DMA((total,)),
            pltpu.SemaphoreType.DMA((total,)),
            pltpu.SemaphoreType.DMA((total,)),
        ],
        compiler_params=pltpu.CompilerParams(
            collective_id=0, has_side_effects=True, vmem_limit_bytes=48 * 1024 * 1024
        ),
    )(tables, index, limits)


def solution(mesh):
    return jax.shard_map(
        shards,
        mesh=mesh,
        in_specs=(
            P(("node", "dev"), None, None),
            P(None, ("node", "dev"), None),
            P(("node", "dev"), None),
        ),
        out_specs=P(("node", "dev"), None, None),
        check_vma=False,
    )
```

time: 92.1 us -> 27.9 us (0.30)
  other arithmetic: 41.8 us -> 0 us
  Pallas kernels: 0 us -> 23.2 us
  blocking collectives: 21.2 us -> 0 us
  matrix products: 9.9 us -> 0 us
  starting transfers between devices: 7.3 us -> 0 us
  local copies, waits for them, and re-layouts: 10.9 us -> 4.54 us
    gather x29 -> x0, other arithmetic: 40.7 us -> none  [shards(): live = local < counts[feature][owner]]
    pallas_call x0 -> x1, Pallas kernels: none -> 23.2 us  [shards(): pl.pallas_call(functools.partial(kernel, groups, members, owned, bagged),...]
    all_to_all x1 -> x0, blocking collectives: 21.2 us -> none  [shards(): lax.all_to_all(outgoing, ('node', 'dev'), split_axis=0, concat_axis=2, ti...]
    dot_general x3 -> x0, matrix products: 9.9 us -> none  [the longest x2 8.78 us: one_block(): jnp.dot(tally.astype(jnp.bfloat16), table, preferred_element_type=jnp.flo...]
    gather x6 -> x0, local copies, waits for them, and re-layouts: 8.06 us -> none  [shards(): live = local < counts[feature][owner]]
    all_to_all x1 -> x0, starting transfers between devices: 7.3 us -> none  [shards(): lax.all_to_all(ids, ('node', 'dev'), split_axis=0, concat_axis=1, tiled=T...]
    unnamed x5 -> x4, local copies, waits for them, and re-layouts: 2.03 us -> 3.41 us
  transfers between devices with their start and end apart: 1 -> 0, of which waited for: 0 -> 0; matrix products, arithmetic and copies ran while one was open for 53% -> 0% of each run, Pallas kernels for 0% -> 0%
where the time goes in v1:
time: 27.9 us; the launch traced here: 27.7 us
  Pallas kernels  23.2 us (83%)
  local copies, waits for them, and re-layouts  4.54 us (16%)
    pallas_call x1, Pallas kernels, shards(): pl.pallas_call(functools.partial(kernel, groups, members, owned, bagged),...  23.2 us
    unnamed x4, local copies, waits for them, and re-layouts  3.41 us
    transpose x1, local copies, waits for them, and re-layouts, shards(): limits = jnp.broadcast_to(counts.T[:, :, None], (total, held, LANES))  0.76 us

profile of v1, /device:TPU:0, one launch (start us, length us, event | category | flops | bytes accessed | tf_op | source)
XLA Modules:
  0.0 27.7 jit_solution(16694176111287673640)
XLA Ops:
  0.0 1.1 %copy.6 = s32[64,16,8]{2,1,0:T(8,128)S(1)} copy(s32[64,16,8]{0,2,1:T(8,128)} %param.4) | data formatting | bytes 65536 | tf_op args[1]
  1.1 0.3 %reshape.4.ids_ref = s32[32,2,128]{2,1,0:T(2,128)S(1)} reshape(s32[64,16,8]{2,1,0:T(8,128)S(1)} %copy.6) | data formatting | bytes 65536 | tf_op jit(solution)/shard_map/reshape | solution.py:181
  1.4 0.8 %copy.7 = s32[32,2]{1,0:T(8,128)S(1)} copy(s32[32,2]{0,1:T(2,128)} %bitcast.1) | data formatting | bytes 512 | tf_op jit(solution)/shard_map/transpose | solution.py:182
  2.2 0.1 broadcast_in_dim.2.counts_ref
  2.3 0.0 copy-start
  2.3 1.6 %copy-done = bf16[2,2048,256]{2,1,0:T(8,128)(2,1)S(1)} copy-done((bf16[2,2048,256]{2,1,0:T(8,128)(2,1)S(1)}, bf16[2,2048,256]{2,1,0:T(8,128)(2,1)}, u32[]{:S(2)}) %copy-start) | copy-done | bytes 2097176
  3.9 23.2 %shard_map.37 = bf16[16,64,64]{2,1,0:T(8,128)(2,1)S(1)} custom-call(bf16[2,2048,256]{2,1,0:T(8,128)(2,1)S(1)} %copy-done, s32[32,2,128]{2,1,0:T(2,128)S(1)} %reshape.4.ids_ref, s32[32,2,128]{2,1,0:T(2,128)S(1)} %broadcast_in_dim.2.counts_ref), custom_call_target="tpu_custom_call" | custom-call | tf_op jit(solution)/shard_map/pallas_call | solution.py:183
  27.0 0.7 %copy.9 = bf16[16,64,64]{2,1,0:T(8,128)(2,1)} copy(bf16[16,64,64]{2,1,0:T(8,128)(2,1)S(1)} %shard_map.37) | data formatting | bytes 262144
Async XLA Ops:
  2.3 1.6 %copy-start = (bf16[2,2048,256]{2,1,0:T(8,128)(2,1)S(1)}, bf16[2,2048,256]{2,1,0:T(8,128)(2,1)}, u32[]{:S(2)}) copy-start(bf16[2,2048,256]{2,1,0:T(8,128)(2,1)} %table_ref.1) | copy-start | bytes 6291460

commit v2 on v1

--- a/solution.py
+++ b/solution.py
@@ -14,12 +14,21 @@
 
 def kernel(
     groups, members, owned, bagged,
-    table_ref, ids_ref, counts_ref, out_ref,
+    table_hbm, ids_hbm, counts_hbm, out_ref,
+    table_ref, ids_in, counts_in, ids_ref, limits,
     id_got, tally, staged, outgoing, received, vectors,
-    id_send, id_recv, row_send, row_recv,
+    table_sem, ids_sem, counts_sem, id_send, id_recv, row_send, row_recv,
 ):
     total = groups * members
     held, height, width = table_ref.shape
+    if groups & (groups - 1):
+        turns = [None] * groups
+    else:
+        turns, bit = [], groups // 2
+        while bit:
+            turns += list(range(bit, 2 * bit))
+            bit //= 2
+        turns.append(0)
     halves = width // LANES
     lines = held * halves * LIVE
     node = lax.axis_index("node")
@@ -49,6 +58,29 @@
             device_id_type=MESH,
         )
 
+    load_ids = pltpu.make_async_copy(ids_hbm, ids_in, ids_sem)
+    load_counts = pltpu.make_async_copy(counts_hbm, counts_in, counts_sem)
+    load_tables = pltpu.make_async_copy(table_hbm, table_ref, table_sem)
+    load_ids.start()
+    load_counts.start()
+    load_tables.start()
+
+    def partner(turn):
+        mask = turns[turn]
+        if mask is None:
+            return lax.rem(node + turn + 1, groups)
+        other, bit = 0, 1
+        while bit < groups:
+            digit = lax.rem(node // bit, 2)
+            other = other + bit * (1 - digit if mask & bit else digit)
+            bit *= 2
+        return other
+
+    def origin(turn):
+        if turns[turn] is None:
+            return lax.rem(node + 2 * groups - turn - 1, groups)
+        return partner(turn)
+
     barrier = pltpu.get_barrier_semaphore()
 
     @pl.loop(1, total)
@@ -56,6 +88,11 @@
         pl.semaphore_signal(
             barrier, inc=1, device_id=place(lax.rem(me + step, total)), device_id_type=MESH
         )
+
+    load_ids.wait()
+    turned = ids_in[...].T
+    for device in range(total):
+        ids_ref[device] = turned[device * held:(device + 1) * held, :]
 
     pl.semaphore_wait(barrier, total - 1)
 
@@ -73,8 +110,16 @@
     on_lane = lax.broadcasted_iota(jnp.int32, (LIVE, members, LANES), 2) // bagged == sample
     rows = LIVE * members
 
+    load_counts.wait()
+    square = (total, total)
+    diagonal = lax.broadcasted_iota(jnp.int32, square, 0) == lax.broadcasted_iota(jnp.int32, square, 1)
+    for feature in range(held):
+        level = counts_in[feature:feature + 1, :].astype(jnp.float32)
+        column = jnp.sum(jnp.where(diagonal, level, 0.0), axis=1, keepdims=True)
+        limits[feature] = jnp.broadcast_to(column, (total, LANES))
+
     for turn in range(groups):
-        group = lax.rem(node + turn + 1, groups)
+        group = partner(turn)
         first = group * members
 
         def wait_ids(member):
@@ -108,10 +153,12 @@
                         piece == number, jnp.ones((), jnp.bfloat16), jnp.zeros((), jnp.bfloat16)
                     )
                 tally[part * 16:(part + 1) * 16, :] = count
+            if turn == 0 and feature == 0:
+                load_tables.wait()
             pooled = jnp.dot(
                 tally[...], table_ref[feature], preferred_element_type=jnp.float32
             )
-            limit = counts_ref[pl.ds(first, members), feature, :]
+            limit = limits[feature, pl.ds(first, members), :]
             for half in range(halves):
                 for s in range(LIVE):
                     piece = pooled[s * members:(s + 1) * members, half * LANES:(half + 1) * LANES]
@@ -134,7 +181,7 @@
     out_ref[LIVE:] = jnp.zeros_like(out_ref[LIVE:])
 
     for turn in range(groups):
-        group = lax.rem(node + 2 * groups - turn - 1, groups)
+        group = origin(turn)
         first = group * members
         if turn < groups - 1:
             @pl.loop(0, members)
@@ -178,29 +225,36 @@
     members = lax.axis_size("dev")
     total = groups * members
     lines = held * (width // LANES) * LIVE
-    index = ids.reshape(total, held, owned * bagged)
-    limits = jnp.broadcast_to(counts.T[:, :, None], (total, held, LANES))
+    index = ids.transpose(1, 2, 0).reshape(owned * bagged, features)
     return pl.pallas_call(
         functools.partial(kernel, groups, members, owned, bagged),
         out_shape=jax.ShapeDtypeStruct((owned, features, features), jnp.bfloat16),
-        in_specs=[pl.BlockSpec(memory_space=pltpu.VMEM)] * 3,
+        in_specs=[pl.BlockSpec(memory_space=pltpu.HBM)] * 3,
         out_specs=pl.BlockSpec(memory_space=pltpu.VMEM),
         scratch_shapes=[
+            pltpu.VMEM(tables.shape, tables.dtype),
+            pltpu.VMEM(index.shape, index.dtype),
+            pltpu.VMEM(counts.shape, counts.dtype),
+            pltpu.VMEM((total, held, LANES), jnp.int32),
+            pltpu.VMEM((held, total, LANES), jnp.float32),
             pltpu.VMEM((total, held, LANES), jnp.int32),
             pltpu.VMEM((LIVE * members, height), jnp.bfloat16),
             pltpu.VMEM((members * lines, LANES), jnp.float32),
             pltpu.VMEM((total, lines, LANES), jnp.bfloat16),
             pltpu.VMEM((total, lines, LANES), jnp.bfloat16),
             pltpu.VMEM((LIVE, width // LANES, groups, members * held, LANES), jnp.float32),
+            pltpu.SemaphoreType.DMA,
+            pltpu.SemaphoreType.DMA,
+            pltpu.SemaphoreType.DMA,
             pltpu.SemaphoreType.DMA((total,)),
             pltpu.SemaphoreType.DMA((total,)),
             pltpu.SemaphoreType.DMA((total,)),
             pltpu.SemaphoreType.DMA((total,)),
         ],
         compiler_params=pltpu.CompilerParams(
-            collective_id=0, has_side_effects=True, vmem_limit_bytes=48 * 1024 * 1024
+            collective_id=0, has_side_effects=True, vmem_limit_bytes=64512 * 1024
         ),
-    )(tables, index, limits)
+    )(tables, index, counts)
 
 
 def solution(mesh):

time: 27.9 us -> 26.2 us (0.939)
  local copies, waits for them, and re-layouts: 4.54 us -> 1.67 us
  Pallas kernels: 23.2 us -> 24.3 us
    unnamed x4 -> x1, local copies, waits for them, and re-layouts: 3.41 us -> 1.67 us
    pallas_call x1, Pallas kernels: 23.2 us -> 24.3 us  [shards(): pl.pallas_call(functools.partial(kernel, groups, members, owned, bagged),...]
    transpose x1 -> x0, local copies, waits for them, and re-layouts: 0.76 us -> none  [shards(): limits = jnp.broadcast_to(counts.T[:, :, None], (total, held, LANES))]
    reshape x1 -> x0, local copies, waits for them, and re-layouts: 0.29 us -> none  [shards(): index = ids.reshape(total, held, owned * bagged)]
where the time goes in v2:
time: 26.2 us; the launch traced here: 26 us
  Pallas kernels  24.3 us (93%)
  local copies, waits for them, and re-layouts  1.67 us (6%)
    pallas_call x1, Pallas kernels, shards(): pl.pallas_call(functools.partial(kernel, groups, members, owned, bagged),...  24.3 us
    unnamed x1, local copies, waits for them, and re-layouts  1.67 us

profile of v2, /device:TPU:0, one launch (start us, length us, event | category | flops | bytes accessed | tf_op | source)
XLA Modules:
  0.0 26.0 jit_solution(17608175196293444141)
XLA Ops:
  0.0 24.3 %shard_map.37 = bf16[16,64,64]{2,1,0:T(8,128)(2,1)} custom-call(bf16[2,2048,256]{2,1,0:T(8,128)(2,1)} %table_hbm.1, s32[128,64]{1,0:T(8,128)} %bitcast.3, s32[2,32]{1,0:T(2,128)} %counts_hbm.1), custom_call_target="tpu_custom_call" | custom-call | tf_op jit(solution)/shard_map/pallas_call | solution.py:229
  24.3 1.7 %copy.5 = bf16[16,64,64]{2,1,0:T(8,128)(2,1)} copy(bf16[16,64,64]{2,1,0:T(8,128)(2,1)} %shard_map.37) | data formatting | bytes 262144

commit v3 on v2

--- a/solution.py
+++ b/solution.py
@@ -96,9 +96,12 @@
 
     pl.semaphore_wait(barrier, total - 1)
 
-    @pl.loop(1, total)
-    def _(step):
-        id_copy(lax.rem(me + step, total), me).start()
+    for turn in range(groups):
+        begin = partner(turn) * members
+
+        @pl.loop(1 if turn == groups - 1 else 0, members, unroll=True)
+        def _(step):
+            id_copy(begin + lax.rem(dev + step, members), me).start()
 
     id_got[me] = ids_ref[me]
 
@@ -126,11 +129,11 @@
             id_copy(first + member, first + member).wait_recv()
 
         if turn < groups - 1:
-            @pl.loop(0, members)
+            @pl.loop(0, members, unroll=True)
             def _(member):
                 wait_ids(member)
         else:
-            @pl.loop(1, members)
+            @pl.loop(1, members, unroll=True)
             def _(step):
                 wait_ids(lax.rem(dev + step, members))
 
@@ -169,11 +172,11 @@
         )
 
         if turn < groups - 1:
-            @pl.loop(0, members)
+            @pl.loop(0, members, unroll=True)
             def _(step):
                 row_copy(first + lax.rem(dev + step, members), me).start()
         else:
-            @pl.loop(1, members)
+            @pl.loop(1, members, unroll=True)
             def _(step):
                 row_copy(first + lax.rem(dev + step, members), me).start()
 
@@ -184,11 +187,11 @@
         group = origin(turn)
         first = group * members
         if turn < groups - 1:
-            @pl.loop(0, members)
+            @pl.loop(0, members, unroll=True)
             def _(member):
                 row_copy(first + member, first + member).wait_recv()
         else:
-            @pl.loop(1, members)
+            @pl.loop(1, members, unroll=True)
             def _(step):
                 source = first + lax.rem(dev + step, members)
                 row_copy(source, source).wait_recv()
@@ -252,9 +255,9 @@
             pltpu.SemaphoreType.DMA((total,)),
         ],
         compiler_params=pltpu.CompilerParams(
-            collective_id=0, has_side_effects=True, vmem_limit_bytes=64512 * 1024
+            collective_id=0, has_side_effects=True, vmem_limit_bytes=48 * 1024 * 1024
         ),
-    )(tables, index, counts)
+    )(*(pltpu.with_memory_space_constraint(x, pltpu.HBM) for x in (tables, index, counts)))
 
 
 def solution(mesh):

time: 26.2 us -> 24 us (0.916)
  Pallas kernels: 24.3 us -> 23.2 us
  local copies, waits for them, and re-layouts: 1.67 us -> 0.71 us
    pallas_call x1, Pallas kernels: 24.3 us -> 23.2 us  [shards(): pl.pallas_call(functools.partial(kernel, groups, members, owned, bagged),...]
    unnamed x1, local copies, waits for them, and re-layouts: 1.67 us -> 0.71 us
where the time goes in v3:
time: 24 us; the launch traced here: 23.9 us
  Pallas kernels  23.2 us (97%)
  local copies, waits for them, and re-layouts  0.71 us (3%)
    pallas_call x1, Pallas kernels, shards(): pl.pallas_call(functools.partial(kernel, groups, members, owned, bagged),...  23.2 us
    unnamed x1, local copies, waits for them, and re-layouts  0.71 us

profile of v3, /device:TPU:0, one launch (start us, length us, event | category | flops | bytes accessed | tf_op | source)
XLA Modules:
  0.0 23.9 jit_solution(11013183785435870060)
XLA Ops:
  0.0 23.2 %shard_map.37 = bf16[16,64,64]{2,1,0:T(8,128)(2,1)S(1)} custom-call(bf16[2,2048,256]{2,1,0:T(8,128)(2,1)} %table_hbm.1, s32[128,64]{1,0:T(8,128)} %bitcast.3, s32[2,32]{1,0:T(2,128)} %counts_hbm.1), custom_call_target="tpu_custom_call" | custom-call | tf_op jit(solution)/shard_map/pallas_call | solution.py:232
  23.2 0.7 %copy.5 = bf16[16,64,64]{2,1,0:T(8,128)(2,1)} copy(bf16[16,64,64]{2,1,0:T(8,128)(2,1)S(1)} %shard_map.37) | data formatting | bytes 262144

commit v4 on v3

--- a/solution.py
+++ b/solution.py
@@ -180,10 +180,19 @@
             def _(step):
                 row_copy(first + lax.rem(dev + step, members), me).start()
 
+    @pl.loop(1, total, unroll=True)
+    def _(step):
+        id_copy(lax.rem(me + step, total), me).wait_send()
+
     received[me] = outgoing[me]
     out_ref[LIVE:] = jnp.zeros_like(out_ref[LIVE:])
 
     for turn in range(groups):
+        if turn == groups - 1:
+            @pl.loop(1, total, unroll=True)
+            def _(step):
+                row_copy(lax.rem(me + step, total), me).wait_send()
+
         group = origin(turn)
         first = group * members
         if turn < groups - 1:
@@ -213,12 +222,6 @@
         out_ref[s] = lax.dot_general(
             mine, mine, (((1,), (1,)), ((), ())), preferred_element_type=jnp.float32
         ).astype(jnp.bfloat16)
-
-    @pl.loop(1, total)
-    def _(step):
-        device = lax.rem(me + step, total)
-        id_copy(device, me).wait_send()
-        row_copy(device, me).wait_send()
 
 
 def shards(tables, ids, counts):

time: 24 us -> 23.7 us (0.987)
  Pallas kernels: 23.2 us -> 22.9 us
    pallas_call x1, Pallas kernels: 23.2 us -> 22.9 us  [shards(): pl.pallas_call(functools.partial(kernel, groups, members, owned, bagged),...]
where the time goes in v4:
time: 23.7 us; the launch traced here: 23.6 us
  Pallas kernels  22.9 us (97%)
  local copies, waits for them, and re-layouts  0.71 us (3%)
    pallas_call x1, Pallas kernels, shards(): pl.pallas_call(functools.partial(kernel, groups, members, owned, bagged),...  22.9 us
    unnamed x1, local copies, waits for them, and re-layouts  0.71 us

profile of v4, /device:TPU:0, one launch (start us, length us, event | category | flops | bytes accessed | tf_op | source)
XLA Modules:
  0.0 23.6 jit_solution(5485003965933740683)
XLA Ops:
  0.0 22.9 %shard_map.37 = bf16[16,64,64]{2,1,0:T(8,128)(2,1)S(1)} custom-call(bf16[2,2048,256]{2,1,0:T(8,128)(2,1)} %table_hbm.1, s32[128,64]{1,0:T(8,128)} %bitcast.3, s32[2,32]{1,0:T(2,128)} %counts_hbm.1), custom_call_target="tpu_custom_call" | custom-call | tf_op jit(solution)/shard_map/pallas_call | solution.py:235
  22.9 0.7 %copy.5 = bf16[16,64,64]{2,1,0:T(8,128)(2,1)} copy(bf16[16,64,64]{2,1,0:T(8,128)(2,1)S(1)} %shard_map.37) | data formatting | bytes 262144
